TPU v7x, 32 devices: a whole 2x2x4 slice. The times are simulated.
32 devices in a mesh: groups: 2 (over x), sub: 16 (over z, y, core).
Axes of the slice: x: 2, y: 2, z: 4, core: 2. Of those that a mesh axis runs over, the one named last changes fastest.
Arguments:
- source_field: float32 [128, 32768], P('groups', 'sub'), parts along dimension 0, may hold values from -6 to 6
- inject_amp: float32 [128], P('groups'), parts along dimension 0, may hold values from 1 to 4
- inject_nodes: int32 [2, 128], P(None, 'groups'), parts along dimension 1, may hold values from 0 to 32767
- node_diag: float32 [32768], P('sub'), may hold values from 3 to 12
- blocks: float32 [256, 7, 128, 128], P('sub'), may hold values from -0.1875 to 0.1875
- pattern: int32 [256, 7], P('sub'), may hold values from 0 to 15
- local_inv: float32 [256, 128, 128], P('sub')
- iface_nodes: int32 [16, 4, 256], P('sub'), may hold values from 0 to 2047
- iface_count: int32 [16, 4], P('sub'), may hold values from 0 to 256, as said below
- iface_wt: float32 [16, 4, 256], P('sub'), may hold values from 0.5 to 2
- aggregate: int32 [32768], P('sub'), may hold values from 0 to 7
- coarse_inv: float32 [128, 128], P('sub')
Outputs:
- solution: float32 [128, 32768], P('groups', 'sub'), parts along dimension 0
- residual: float32 [128, 32768], P('groups', 'sub'), parts along dimension 0
There are 2 independent parts, one for each index of `groups`. A program takes and returns all parts, laid end to end along the dimension named above; an argument that names none is the same for every part. Nothing has to cross between parts.
Inputs may be any that keep to these rules, and one draw needn't show every extreme that they name: `iface_count`: for the two subdomains of a pair the counts of their facing slots are equal; counts toward subdomains outside the mesh are 0; some pair uses all 256 slots.
All inputs are finite; a program needn't handle non-finite values.
Results may differ from a plain program's by a relative error of at most 0.00012.
Values sent between devices are 32-bit elements; how exact they have to be, the bound alone decides.
A program may use at most 64 MiB of HBM per device.

v0:
```python
import functools
import jax
import jax.numpy as jnp
from jax import lax
from jax.experimental import pallas as pl
from jax.experimental.pallas import tpu as pltpu
from jax.sharding import PartitionSpec as P

ITERS = 3
OFFSETS = (-2, -1, 1, 2)
EPSILON = 1e-06
HIGH = lax.Precision.HIGHEST
F32 = jnp.float32
BF16 = jnp.bfloat16
NT = (((1,), (1,)), ((), ()))


def split(value):
    high = value.astype(BF16)
    low = (value - high.astype(F32)).astype(BF16)
    return jnp.concatenate([high, low], axis=0)


def nt_dot(left, right):
    return lax.dot_general(left, right, NT, preferred_element_type=F32)


def fold(product, columns, width):
    return (
        product[:columns, :width]
        + product[:columns, width:]
        + product[columns : 2 * columns, :width]
    )


def kernel(
    source_ref,
    amp_ref,
    inject_ref,
    diag_ref,
    blocks_hbm,
    pattern_ref,
    inverse_hbm,
    nodes_ref,
    count_ref,
    weight_ref,
    aggregate_ref,
    coarse_ref,
    x_ref,
    r_ref,
    raw,
    raw_inv,
    mat,
    inv,
    onehot,
    split_v,
    split_l,
    member,
    extra,
    local,
    upd,
    img,
    out_y,
    ap,
    scaled,
    tile,
    near_inv,
    sums,
    outbox,
    inbox,
    raw_sem,
    inv_sem,
    sum_send,
    sum_recv,
    face_send,
    face_recv,
    near_send,
    near_recv,
):
    n_sub = lax.axis_size("sub")
    me = lax.axis_index("sub")
    columns, node_count = source_ref.shape
    rows, kept, size, _ = blocks_hbm.shape
    agg = coarse_ref.shape[0]
    slots = nodes_ref.shape[2]
    double = 2 * columns
    near = [me + offset for offset in OFFSETS]
    there = [jnp.logical_and(other >= 0, other < n_sub) for other in near]

    barrier = pltpu.get_barrier_semaphore()

    def greet(step, carry):
        other = lax.rem(me + step, n_sub)
        pl.semaphore_signal(
            barrier, inc=1, device_id={"sub": other}, device_id_type=pl.DeviceIdType.MESH
        )
        return carry

    def inverse_copy():
        return pltpu.make_async_copy(inverse_hbm, raw_inv, inv_sem)

    def block_copy(i):
        return pltpu.make_async_copy(blocks_hbm.at[i], raw.at[i], raw_sem.at[i])

    inverse_copy().start()
    for i in range(rows):
        block_copy(i).start()

    inbox[...] = jnp.zeros_like(inbox)
    near_inv[...] = jnp.zeros_like(near_inv)
    near_inv[0:agg, :] = coarse_ref[...]
    lax.fori_loop(1, n_sub, greet, 0)

    tile[...] = jnp.zeros_like(tile)
    tile[0:2, 0:columns] = inject_ref[...].astype(F32)
    tile[2:3, 0:columns] = amp_ref[...]
    turned = tile[...].T
    first_node = me * node_count
    at_source = turned[:columns, 0:1].astype(jnp.int32) - first_node
    at_sink = turned[:columns, 1:2].astype(jnp.int32) - first_node
    amp = turned[:columns, 2:3]
    lane = lax.broadcasted_iota(jnp.int32, (columns, size), 1)
    agg_id = lax.broadcasted_iota(jnp.int32, (2 * agg, size), 0)
    for i in range(rows):
        place = slice(i * size, (i + 1) * size)
        node = lane + i * size
        hits = (node == at_source).astype(F32) - (node == at_sink).astype(F32)
        rhs = source_ref[:, place] + amp * hits
        out_y[i] = rhs
        split_v[:, place] = split(rhs)
        belongs = (agg_id == aggregate_ref[:, place]).astype(F32).astype(BF16)
        member[:, place] = belongs
        split_l[i, double : double + 2 * agg, :] = belongs

    pl.semaphore_wait(barrier, n_sub - 1)

    def sum_copy(stage, other):
        return pltpu.make_async_remote_copy(
            src_ref=sums.at[stage, me],
            dst_ref=sums.at[stage, me],
            send_sem=sum_send.at[stage],
            recv_sem=sum_recv.at[stage],
            device_id={"sub": other},
            device_id_type=pl.DeviceIdType.MESH,
        )

    def send_sums(stage):
        def one(step, carry):
            sum_copy(stage, lax.rem(me + step, n_sub)).start()
            return carry

        lax.fori_loop(1, n_sub, one, 0)

    def all_sums(stage, sem):
        span = sums.at[stage, pl.ds(0, n_sub - 1)]
        return pltpu.make_async_copy(span, span, sem.at[stage])

    def face_copy(stage, j):
        depth = columns + agg if stage == 0 else columns
        return pltpu.make_async_remote_copy(
            src_ref=outbox.at[stage, j, pl.ds(0, depth)],
            dst_ref=inbox.at[stage, 3 - j, pl.ds(0, depth)],
            send_sem=face_send.at[stage, j],
            recv_sem=face_recv.at[stage, 3 - j],
            device_id={"sub": near[j]},
            device_id_type=pl.DeviceIdType.MESH,
        )

    def face_arrival(stage, j):
        depth = columns + agg if stage == 0 else columns
        span = inbox.at[stage, j, pl.ds(0, depth)]
        return pltpu.make_async_copy(span, span, face_recv.at[stage, j])

    def near_copy(j):
        return pltpu.make_async_remote_copy(
            src_ref=coarse_ref,
            dst_ref=near_inv.at[pl.ds((4 - j) * agg, agg)],
            send_sem=near_send.at[j],
            recv_sem=near_recv.at[3 - j],
            device_id={"sub": near[j]},
            device_id_type=pl.DeviceIdType.MESH,
        )

    def near_arrival(j):
        span = near_inv.at[pl.ds((1 + j) * agg, agg)]
        return pltpu.make_async_copy(span, span, near_recv.at[j])

    def put_dots():
        def add(i, carry):
            image = img[i]
            return carry[0] + r_now(i) * image, carry[1] + image * image

        zero = jnp.zeros((columns, size), F32)
        ri, ii = lax.fori_loop(0, rows, add, (zero, zero))
        turned = jnp.concatenate([ri, ii], axis=0).T
        return jnp.sum(turned.reshape(size // 8, 8, double), axis=0)

    def r_now(i):
        return out_r[i]

    def step_of(stage):
        total = jnp.sum(sums[stage, :, 8:16, :], axis=(0, 1), keepdims=False)[None, :]
        both = jnp.broadcast_to(total, (size, double)).T
        return both[:columns] / (both[columns:] + EPSILON)

    out_r, y_now, x_now = upd.at[1], upd.at[2], upd.at[3]
    u_now = upd.at[0]

    def keep_rhs(i, carry):
        out_r[i] = out_y[i]
        return carry

    lax.fori_loop(0, rows, keep_rhs, 0)

    for stage in range(ITERS):
        sums[stage, me, 0:8, :] = nt_dot(member[...], split_v[...])[:agg]
        if stage:
            sums[stage, me, 8:16, :] = put_dots()
        else:
            sums[stage, me, 8:16, :] = jnp.zeros((8, double), F32)
        send_sums(stage)
        if stage == 0:
            for j in range(4):
                pl.when(there[j])(near_copy(j).start)
            for j in range(4):
                live = lax.broadcasted_iota(jnp.int32, (1, slots), 1) < count_ref[0, j]
                scaled[:, j * slots : (j + 1) * slots] = jnp.where(
                    live, weight_ref[0, j : j + 1, :], 0.0
                )
            span = 2 * size

            def build(c, carry):
                ids = lax.broadcasted_iota(jnp.int32, (span, slots), 0) + c * span
                for j in range(4):
                    same = ids == nodes_ref[0, j : j + 1, :]
                    onehot[
                        pl.ds(pl.multiple_of(c * span, span), span),
                        j * slots : (j + 1) * slots,
                    ] = jnp.where(same, 1.0, 0.0).astype(BF16)
                return carry

            lax.fori_loop(0, rows // 2, build, 0)
            inverse_copy().wait()

        def solve(half, carry):
            for part in range(2):
                i = 2 * half + part
                if stage == 0:
                    inv[i] = split(raw_inv[i])
                place = pl.ds(pl.multiple_of(i * size, size), size)
                value = fold(nt_dot(split_v[:, place], inv[i]), columns, size)
                local[i] = value
                split_l[i, 0:double, :] = split(value)
            return carry

        lax.fori_loop(0, rows // 2, solve, 0)

        depth = double + 2 * agg if stage == 0 else double
        left = jnp.concatenate([split_l[i, 0:depth, :] for i in range(rows)], axis=1)
        for j in range(4):
            got = jnp.dot(
                left, onehot[:, j * slots : (j + 1) * slots], preferred_element_type=F32
            )
            outbox[stage, j, 0:columns, :] = got[:columns] + got[columns:double]
            if stage == 0:
                outbox[stage, j, columns : columns + agg, :] = got[double : double + agg]
            pl.when(there[j])(face_copy(stage, j).start)

        def apply(half, carry):
            for part in range(2):
                i = 2 * half + part
                if stage == 0:
                    block_copy(i).wait()
                    for k in range(kept):
                        mat[i, :, k * size : (k + 1) * size] = split(raw[i, k])
                picked = jnp.concatenate(
                    [split_l[pattern_ref[i, k], 0:depth, :] for k in range(kept)], axis=1
                )
                product = nt_dot(picked, mat[i])
                place = pl.ds(pl.multiple_of(i * size, size), size)
                diag = diag_ref[:, place]
                y_now[i] = fold(product, columns, size) + diag * local[i]
                if stage == 0:
                    own = product[double : double + agg]
                    mine = split_l[i, double : double + 2 * agg, :].astype(F32)[:agg]
                    ap[i, 0:agg, :] = own[:, :size] + own[:, size:] + diag * mine
            return carry

        lax.fori_loop(0, rows // 2, apply, 0)

        for j in range(4):
            pl.when(there[j])(face_arrival(stage, j).wait)
        pieces = [
            split(inbox[stage, j, 0:columns, :] * scaled[:, j * slots : (j + 1) * slots])
            for j in range(4)
        ]
        left = jnp.concatenate(pieces, axis=1)
        if stage == 0:
            strips = []
            for j in range(4):
                strip = inbox[stage, j, columns : columns + agg, :]
                strip = strip * scaled[:, j * slots : (j + 1) * slots]
                cells = [jnp.zeros((agg, slots), F32)] * 4
                cells[j] = strip
                strips.append(jnp.concatenate(cells, axis=1))
            left = jnp.concatenate([left, split(jnp.concatenate(strips, axis=0))], axis=0)

        def scatter(c, carry):
            span = 2 * size
            chunk = onehot[pl.ds(pl.multiple_of(c * span, span), span), :]
            product = nt_dot(left, chunk)
            for part in range(2):
                piece = product[:, part * size : (part + 1) * size]
                i = 2 * c + part
                y_now[i] = y_now[i] - (piece[:columns] + piece[columns:double])
                if stage == 0:
                    outer = piece[double : double + 4 * agg] + piece[double + 4 * agg :]
                    ap[i, agg : 5 * agg, :] = -outer
                    high = ap[i].astype(BF16).astype(F32)
                    low = ap[i] - high
                    pad = jnp.zeros((agg, size), F32)
                    tail = jnp.zeros((size - 11 * agg, size), F32)
                    extra[i, :, 0:size] = jnp.concatenate(
                        [high, pad, low, tail], axis=0
                    ).astype(BF16)
                    mine = split_l[i, double : double + 2 * agg, :].astype(F32)[:agg]
                    extra[i, :, size : 2 * size] = jnp.concatenate(
                        [mine, jnp.zeros((size - agg, size), F32)], axis=0
                    ).astype(BF16)
            return carry

        lax.fori_loop(0, rows // 2, scatter, 0)

        all_sums(stage, sum_recv).wait()
        if stage == 0:
            for j in range(4):
                pl.when(there[j])(near_arrival(j).wait)
        gathered = sums[stage, :, 0:8, :].reshape(n_sub * agg, double)
        coarse = jnp.dot(near_inv[...], gathered, precision=HIGH, preferred_element_type=F32)
        turned = jnp.concatenate(
            [coarse, jnp.zeros((agg, double), F32), coarse, jnp.zeros((size - 11 * agg, double), F32)],
            axis=0,
        ).T
        coarse_split = split(turned[:columns] + turned[columns:])
        if stage:
            step = step_of(stage)

        def finish(half, carry):
            for part in range(2):
                i = 2 * half + part
                product = jnp.dot(coarse_split, extra[i], preferred_element_type=F32)
                product = product[:columns] + product[columns:]
                image = y_now[i] + product[:, :size]
                update = local[i] + product[:, size:]
                if stage == 0:
                    new_u, new_w = update, image
                    x_now[i] = jnp.zeros_like(update)
                else:
                    old_u, old_w = u_now[i], img[i]
                    x_now[i] = x_now[i] + step * old_u
                    out_r[i] = out_r[i] - step * old_w
                    new_u, new_w = old_u - step * update, old_w - step * image
                u_now[i] = new_u
                img[i] = new_w
                if stage < ITERS - 1:
                    place = pl.ds(pl.multiple_of(i * size, size), size)
                    split_v[:, place] = split(new_w)
            return carry

        lax.fori_loop(0, rows // 2, finish, 0)

    sums[ITERS, me, 0:8, :] = jnp.zeros((8, double), F32)
    sums[ITERS, me, 8:16, :] = put_dots()
    send_sums(ITERS)
    all_sums(ITERS, sum_recv).wait()
    step = step_of(ITERS)
    for i in range(rows):
        place = slice(i * size, (i + 1) * size)
        x_ref[:, place] = x_now[i] + step * u_now[i]
        r_ref[:, place] = out_r[i] - step * img[i]

    for stage in range(ITERS + 1):
        all_sums(stage, sum_send).wait()
    for j in range(4):
        pl.when(there[j])(near_copy(j).wait_send)
        for stage in range(ITERS):
            pl.when(there[j])(face_copy(stage, j).wait_send)


def shards(
    source_field,
    inject_amp,
    inject_nodes,
    node_diag,
    blocks,
    pattern,
    local_inv,
    iface_nodes,
    iface_count,
    iface_wt,
    aggregate,
    coarse_inv,
):
    columns, node_count = source_field.shape
    rows, kept, size, _ = blocks.shape
    agg, n_coarse = coarse_inv.shape
    slots = iface_wt.shape[2]
    n_sub = lax.axis_size("sub")
    vmem = pl.BlockSpec(memory_space=pltpu.VMEM)
    smem = pl.BlockSpec(memory_space=pltpu.SMEM)
    far = pl.BlockSpec(memory_space=pl.ANY)
    field = jax.ShapeDtypeStruct((columns, node_count), F32)
    dma = pltpu.SemaphoreType.DMA
    return pl.pallas_call(
        kernel,
        out_shape=(field, field),
        in_specs=[vmem, vmem, vmem, vmem, far, smem, far, vmem, smem, vmem, vmem, vmem],
        out_specs=(vmem, vmem),
        scratch_shapes=[
            pltpu.VMEM((rows, kept, size, size), F32),
            pltpu.VMEM((rows, size, size), F32),
            pltpu.VMEM((rows, 2 * size, kept * size), BF16),
            pltpu.VMEM((rows, 2 * size, size), BF16),
            pltpu.VMEM((node_count, 4 * slots), BF16),
            pltpu.VMEM((2 * columns, node_count), BF16),
            pltpu.VMEM((rows, 2 * columns + 2 * agg, size), BF16),
            pltpu.VMEM((2 * agg, node_count), BF16),
            pltpu.VMEM((rows, size, 2 * size), BF16),
            pltpu.VMEM((rows, columns, size), F32),
            pltpu.VMEM((4, rows, columns, size), F32),
            pltpu.VMEM((rows, columns, size), F32),
            pltpu.VMEM((rows, columns, size), F32),
            pltpu.VMEM((rows, 5 * agg, size), F32),
            pltpu.VMEM((1, 4 * slots), F32),
            pltpu.VMEM((size, size), F32),
            pltpu.VMEM((5 * agg, n_coarse), F32),
            pltpu.VMEM((ITERS + 1, n_sub, 16, 2 * columns), F32),
            pltpu.VMEM((ITERS, 4, columns + agg, slots), F32),
            pltpu.VMEM((ITERS, 4, columns + agg, slots), F32),
            dma((rows,)),
            dma,
            dma((ITERS + 1,)),
            dma((ITERS + 1,)),
            dma((ITERS, 4)),
            dma((ITERS, 4)),
            dma((4,)),
            dma((4,)),
        ],
        compiler_params=pltpu.CompilerParams(
            collective_id=0, has_side_effects=True, vmem_limit_bytes=56 * 1024 * 1024
        ),
        cost_estimate=pl.CostEstimate(
            flops=4_000_000_000, bytes_accessed=12_000_000, transcendentals=0
        ),
    )(
        source_field,
        inject_amp.reshape(1, columns),
        inject_nodes,
        node_diag.reshape(1, node_count),
        blocks,
        pattern,
        local_inv,
        iface_nodes,
        iface_count,
        iface_wt,
        aggregate.reshape(1, node_count),
        coarse_inv,
    )


def solution(mesh):
    in_specs = (
        P("groups", "sub"),
        P("groups"),
        P(None, "groups"),
        P("sub"),
        P("sub", None, None, None),
        P("sub", None),
        P("sub", None, None),
        P("sub", None, None),
        P("sub", None),
        P("sub", None, None),
        P("sub"),
        P("sub", None),
    )
    out_specs = (P("groups", "sub"), P("groups", "sub"))
    return jax.shard_map(shards, mesh=mesh, in_specs=in_specs, out_specs=out_specs, check_vma=False)
```

profile of v0, /device:TPU:0, one launch (start us, length us, event | category | flops | bytes accessed | tf_op | source)
XLA Modules:
  0.0 60.8 jit_solution(18265894700854814124)
XLA Ops:
  0.6 1.4 %copy.14.pattern_ref = s32[16,7]{1,0:T(8,128)} copy(s32[16,7]{0,1:T(8,128)} %param.17) | data formatting | bytes 896 | tf_op args[5]
  2.0 55.0 %shard_map.131 = (f32[64,2048]{1,0:T(8,128)}, f32[64,2048]{1,0:T(8,128)}) custom-call(f32[64,2048]{1,0:T(8,128)} %source_ref.1, f32[1,64]{1,0:T(1,128)} %bitcast.5, s32[2,64]{1,0:T(2,128)} %inject_ref.1, f32[1,2048]{1,0:T(1,128)} %bitcast.3, f32[16,7,128,128]{3,2,1,0:T(8,128)} %blocks_hbm.1, s32[16,7]{1,0:T(8,128)} %copy.14.pattern_ref, ...), custom_call_target="tpu_custom_call" | custom-call | flops 4000000000 | bytes 12000000 | tf_op jit(solution)/shard_map/pallas_call | solution.py:414
  57.0 1.9 %copy.17 = f32[64,2048]{1,0:T(8,128)} copy(f32[64,2048]{1,0:T(8,128)} %get-tuple-element.4) | data formatting | bytes 1048576
  58.9 1.9 %copy.18 = f32[64,2048]{1,0:T(8,128)} copy(f32[64,2048]{1,0:T(8,128)} %get-tuple-element.5) | data formatting | bytes 1048576
where the time goes:
time: 61 us; the launch traced here: 60.8 us
  Pallas kernels  55 us (90%)
  local copies, waits for them, and re-layouts  5.11 us (8%)
  between operations  0.64 us (1%)
    pallas_call x1, Pallas kernels, shards(): pl.pallas_call(kernel, out_shape=(field, field), in_specs=[vmem, vmem, vm...  55 us
    unnamed x3, local copies, waits for them, and re-layouts  5.11 us

commit v1 on v0

v1 whole, which is shorter than its diff:
```python
import functools
import jax
import jax.numpy as jnp
from jax import lax
from jax.experimental import pallas as pl
from jax.experimental.pallas import tpu as pltpu
from jax.sharding import PartitionSpec as P

ITERS = 3
OFFSETS = (-2, -1, 1, 2)
EPSILON = 1e-06
HIGH = lax.Precision.HIGHEST
F32 = jnp.float32
BF16 = jnp.bfloat16
NT = (((1,), (1,)), ((), ()))


def split(value):
    high = value.astype(BF16)
    low = (value - high.astype(F32)).astype(BF16)
    return jnp.concatenate([high, low], axis=0)


def nt_dot(left, right):
    return lax.dot_general(left, right, NT, preferred_element_type=F32)


def fold(product, columns, width):
    return (
        product[:columns, :width]
        + product[:columns, width:]
        + product[columns : 2 * columns, :width]
    )


def kernel(
    source_hbm,
    amp_ref,
    inject_ref,
    diag_ref,
    blocks_hbm,
    pattern_hbm,
    inverse_hbm,
    nodes_ref,
    count_ref,
    weight_ref,
    aggregate_ref,
    coarse_ref,
    x_hbm,
    u_hbm,
    r_hbm,
    w_hbm,
    step_ref,
    raw,
    raw_inv,
    mat,
    inv,
    onehot,
    split_v,
    split_l,
    member,
    extra,
    local,
    x_now,
    u_now,
    r_now,
    w_now,
    y_now,
    ap,
    scaled,
    tile,
    near_inv,
    sums,
    outbox,
    inbox,
    pattern_ref,
    load_sem,
    raw_sem,
    out_sem,
    sum_send,
    sum_recv,
    face_send,
    face_recv,
    near_send,
    near_recv,
):
    n_sub = lax.axis_size("sub")
    me = lax.axis_index("sub")
    columns, node_count = r_now.shape
    rows, kept, size, _ = blocks_hbm.shape
    agg = coarse_ref.shape[0]
    slots = nodes_ref.shape[2]
    double = 2 * columns
    near = [me + offset for offset in OFFSETS]
    there = [jnp.logical_and(other >= 0, other < n_sub) for other in near]

    def each(count, body, init=0):
        return lax.fori_loop(0, count, body, init, unroll=True)

    def others(body):
        def one(step, carry):
            body(lax.rem(me + step, n_sub))
            return carry

        lax.fori_loop(1, n_sub, one, 0, unroll=n_sub <= 16)

    def at(i):
        return pl.ds(pl.multiple_of(i * size, size), size)

    barrier = pltpu.get_barrier_semaphore()

    def greet(other):
        pl.semaphore_signal(
            barrier, inc=1, device_id={"sub": other}, device_id_type=pl.DeviceIdType.MESH
        )

    def block_copy(i):
        return pltpu.make_async_copy(blocks_hbm.at[i], raw.at[i], raw_sem.at[i])

    source_copy = pltpu.make_async_copy(source_hbm, r_now, load_sem.at[0])
    inverse_copy = pltpu.make_async_copy(inverse_hbm, raw_inv, load_sem.at[1])
    pattern_copy = pltpu.make_async_copy(pattern_hbm, pattern_ref, load_sem.at[2])
    source_copy.start()
    inverse_copy.start()
    pattern_copy.start()
    for i in range(rows):
        block_copy(i).start()
    others(greet)

    near_inv[0:agg, :] = coarse_ref[...]

    def blank(j):
        inbox[:, j] = jnp.zeros((ITERS,) + inbox.shape[2:], F32)
        near_inv[(1 + j) * agg : (2 + j) * agg, :] = jnp.zeros((agg, near_inv.shape[1]), F32)

    for j in range(4):
        pl.when(jnp.logical_not(there[j]))(functools.partial(blank, j))

    for j in range(4):
        live = lax.broadcasted_iota(jnp.int32, (1, slots), 1) < count_ref[0, j]
        scaled[:, j * slots : (j + 1) * slots] = jnp.where(
            live, weight_ref[0, j : j + 1, :], 0.0
        )
    span = 2 * size

    def build(c, carry):
        ids = lax.broadcasted_iota(jnp.int32, (span, slots), 0) + c * span
        for j in range(4):
            same = ids == nodes_ref[0, j : j + 1, :]
            onehot[
                pl.ds(pl.multiple_of(c * span, span), span), j * slots : (j + 1) * slots
            ] = jnp.where(same, 1.0, 0.0).astype(BF16)
        return carry

    lax.fori_loop(0, rows // 2, build, 0)

    tile[...] = jnp.zeros_like(tile)
    tile[0:2, 0:columns] = inject_ref[...].astype(F32)
    tile[2:3, 0:columns] = amp_ref[...]
    turned = tile[...].T
    first_node = me * node_count
    at_source = turned[:columns, 0:1].astype(jnp.int32) - first_node
    at_sink = turned[:columns, 1:2].astype(jnp.int32) - first_node
    amp = turned[:columns, 2:3]
    lane = lax.broadcasted_iota(jnp.int32, (columns, size), 1)
    agg_id = lax.broadcasted_iota(jnp.int32, (2 * agg, size), 0)
    source_copy.wait()
    for i in range(rows):
        place = slice(i * size, (i + 1) * size)
        node = lane + i * size
        hits = (node == at_source).astype(F32) - (node == at_sink).astype(F32)
        rhs = r_now[:, place] + amp * hits
        r_now[:, place] = rhs
        split_v[:, place] = split(rhs)
        belongs = (agg_id == aggregate_ref[:, place]).astype(F32).astype(BF16)
        member[:, place] = belongs
        split_l[i, double : double + 2 * agg, :] = belongs

    def sum_copy(stage, other):
        return pltpu.make_async_remote_copy(
            src_ref=sums.at[stage, me],
            dst_ref=sums.at[stage, me],
            send_sem=sum_send.at[stage],
            recv_sem=sum_recv.at[stage],
            device_id={"sub": other},
            device_id_type=pl.DeviceIdType.MESH,
        )

    def send_sums(stage):
        others(lambda other: sum_copy(stage, other).start())

    def all_sums(stage, sem):
        part = sums.at[stage, pl.ds(0, n_sub - 1)]
        return pltpu.make_async_copy(part, part, sem.at[stage])

    def face_copy(stage, j):
        depth = columns + agg if stage == 0 else columns
        return pltpu.make_async_remote_copy(
            src_ref=outbox.at[stage, j, pl.ds(0, depth)],
            dst_ref=inbox.at[stage, 3 - j, pl.ds(0, depth)],
            send_sem=face_send.at[stage, j],
            recv_sem=face_recv.at[stage, 3 - j],
            device_id={"sub": near[j]},
            device_id_type=pl.DeviceIdType.MESH,
        )

    def face_arrival(stage, j):
        depth = columns + agg if stage == 0 else columns
        part = inbox.at[stage, j, pl.ds(0, depth)]
        return pltpu.make_async_copy(part, part, face_recv.at[stage, j])

    def near_copy(j):
        return pltpu.make_async_remote_copy(
            src_ref=coarse_ref,
            dst_ref=near_inv.at[pl.ds((4 - j) * agg, agg)],
            send_sem=near_send.at[j],
            recv_sem=near_recv.at[3 - j],
            device_id={"sub": near[j]},
            device_id_type=pl.DeviceIdType.MESH,
        )

    def near_arrival(j):
        part = near_inv.at[pl.ds((1 + j) * agg, agg)]
        return pltpu.make_async_copy(part, part, near_recv.at[j])

    def dots_tile(dots):
        turned = jnp.concatenate(dots, axis=0).T
        part = jnp.sum(turned.reshape(size // 4, 4, double), axis=0)
        return jnp.concatenate([part[:, :columns], part[:, columns:]], axis=0)

    def step_of(stage):
        total = jnp.sum(sums[stage], axis=0)[:, columns:]
        top = jnp.sum(total[0:4], axis=0, keepdims=True)
        bottom = jnp.sum(total[4:8], axis=0, keepdims=True)
        line = top / (bottom + EPSILON)
        line = jnp.concatenate([line, line], axis=1)
        return jnp.broadcast_to(line, (size, double)).T[:columns]

    zero = jnp.zeros((columns, size), F32)
    dots = None
    pl.semaphore_wait(barrier, n_sub - 1)

    for stage in range(ITERS):
        coarse = nt_dot(member[...], split_v[...])[:agg]
        beside = dots_tile(dots) if stage else jnp.zeros((agg, columns), F32)
        sums[stage, me] = jnp.concatenate(
            [coarse[:, :columns] + coarse[:, columns:], beside], axis=1
        )
        send_sums(stage)
        if stage == 0:
            for j in range(4):
                pl.when(there[j])(near_copy(j).start)
            inverse_copy.wait()

        def solve(i, carry):
            if stage == 0:
                inv[i] = split(raw_inv[i])
            value = fold(nt_dot(split_v[:, at(i)], inv[i]), columns, size)
            local[:, at(i)] = value
            split_l[i, 0:double, :] = split(value)
            return carry

        each(rows, solve)

        depth = double + 2 * agg if stage == 0 else double
        left = jnp.concatenate([split_l[i, 0:depth, :] for i in range(rows)], axis=1)
        for j in range(4):
            got = jnp.dot(
                left, onehot[:, j * slots : (j + 1) * slots], preferred_element_type=F32
            )
            outbox[stage, j, 0:columns, :] = got[:columns] + got[columns:double]
            if stage == 0:
                outbox[stage, j, columns : columns + agg, :] = got[double : double + agg]
            pl.when(there[j])(face_copy(stage, j).start)
        if stage == 0:
            pattern_copy.wait()

        def apply(i, carry):
            if stage == 0:
                block_copy(i).wait()
                for k in range(kept):
                    mat[i, :, k * size : (k + 1) * size] = split(raw[i, k])
            picked = jnp.concatenate(
                [split_l[pattern_ref[i, k], 0:depth, :] for k in range(kept)], axis=1
            )
            product = nt_dot(picked, mat[i])
            diag = diag_ref[:, at(i)]
            y_now[:, at(i)] = fold(product, columns, size) + diag * local[:, at(i)]
            if stage == 0:
                own = product[double : double + agg]
                mine = split_l[i, double : double + 2 * agg, :].astype(F32)[:agg]
                ap[i, 0:agg, :] = own[:, :size] + own[:, size:] + diag * mine
            return carry

        each(rows, apply)

        all_sums(stage, sum_recv).wait()
        for j in range(4):
            if stage == 0:
                pl.when(there[j])(near_arrival(j).wait)
            pl.when(there[j])(face_arrival(stage, j).wait)

        gathered = sums[stage].reshape(n_sub * agg, double)
        coarse = jnp.dot(near_inv[...], gathered, precision=HIGH, preferred_element_type=F32)
        gap = jnp.zeros((agg, double), F32)
        tail = jnp.zeros((size - 11 * agg, double), F32)
        coarse_split = split(jnp.concatenate([coarse, gap, coarse, tail], axis=0).T[:columns])
        if stage:
            step = step_of(stage)

        pieces = [
            split(inbox[stage, j, 0:columns, :] * scaled[:, j * slots : (j + 1) * slots])
            for j in range(4)
        ]
        left = jnp.concatenate(pieces, axis=1)
        if stage == 0:
            strips = []
            for j in range(4):
                strip = inbox[stage, j, columns : columns + agg, :]
                strip = strip * scaled[:, j * slots : (j + 1) * slots]
                cells = [jnp.zeros((agg, slots), F32)] * 4
                cells[j] = strip
                strips.append(jnp.concatenate(cells, axis=1))
            left = jnp.concatenate([left, split(jnp.concatenate(strips, axis=0))], axis=0)

        def finish(c, dots):
            chunk = onehot[pl.ds(pl.multiple_of(c * span, span), span), :]
            scattered = nt_dot(left, chunk)
            for part in range(2):
                i = 2 * c + part
                piece = scattered[:, part * size : (part + 1) * size]
                if stage == 0:
                    outer = piece[double : double + 4 * agg] + piece[double + 4 * agg :]
                    ap[i, agg : 5 * agg, :] = -outer
                    high = ap[i].astype(BF16).astype(F32)
                    low = ap[i] - high
                    pad = jnp.zeros((agg, size), F32)
                    end = jnp.zeros((size - 11 * agg, size), F32)
                    extra[i, :, 0:size] = jnp.concatenate([high, pad, low, end], axis=0).astype(BF16)
                    mine = split_l[i, double : double + 2 * agg, :].astype(F32)[:agg]
                    extra[i, :, size : 2 * size] = jnp.concatenate(
                        [mine, jnp.zeros((size - agg, size), F32)], axis=0
                    ).astype(BF16)
                product = jnp.dot(coarse_split, extra[i], preferred_element_type=F32)
                product = product[:columns] + product[columns:]
                image = y_now[:, at(i)] - (piece[:columns] + piece[columns:double])
                image = image + product[:, :size]
                update = local[:, at(i)] + product[:, size:]
                residual = r_now[:, at(i)]
                if stage:
                    old_u, old_w = u_now[:, at(i)], w_now[:, at(i)]
                    advance = step * old_u
                    x_now[:, at(i)] = advance if stage == 1 else x_now[:, at(i)] + advance
                    residual = residual - step * old_w
                    r_now[:, at(i)] = residual
                    update, image = old_u - step * update, old_w - step * image
                u_now[:, at(i)] = update
                w_now[:, at(i)] = image
                if stage < ITERS - 1:
                    split_v[:, at(i)] = split(image)
                dots = [dots[0] + residual * image, dots[1] + image * image]
            return dots

        dots = each(rows // 2, finish, [zero, zero])

    sums[ITERS, me] = jnp.concatenate([jnp.zeros((agg, columns), F32), dots_tile(dots)], axis=1)
    send_sums(ITERS)
    leaving = [
        pltpu.make_async_copy(held, out, out_sem.at[place])
        for place, (held, out) in enumerate(
            ((x_now, x_hbm), (u_now, u_hbm), (r_now, r_hbm), (w_now, w_hbm))
        )
    ]
    for copy in leaving:
        copy.start()
    for j in range(4):
        pl.when(there[j])(near_copy(j).wait_send)
        for stage in range(ITERS):
            pl.when(there[j])(face_copy(stage, j).wait_send)
    for stage in range(ITERS + 1):
        all_sums(stage, sum_send).wait()
    all_sums(ITERS, sum_recv).wait()
    step_ref[...] = step_of(ITERS)
    for copy in leaving:
        copy.wait()


def shards(
    source_field,
    inject_amp,
    inject_nodes,
    node_diag,
    blocks,
    pattern,
    local_inv,
    iface_nodes,
    iface_count,
    iface_wt,
    aggregate,
    coarse_inv,
):
    columns, node_count = source_field.shape
    rows, kept, size, _ = blocks.shape
    agg, n_coarse = coarse_inv.shape
    slots = iface_wt.shape[2]
    n_sub = lax.axis_size("sub")
    vmem = pl.BlockSpec(memory_space=pltpu.VMEM)
    smem = pl.BlockSpec(memory_space=pltpu.SMEM)
    far = pl.BlockSpec(memory_space=pl.ANY)
    field = jax.ShapeDtypeStruct((columns, node_count), F32)
    held = pltpu.VMEM((columns, node_count), F32)
    dma = pltpu.SemaphoreType.DMA
    x, u, r, w, step = pl.pallas_call(
        kernel,
        out_shape=(field, field, field, field, jax.ShapeDtypeStruct((columns, size), F32)),
        in_specs=[far, vmem, vmem, vmem, far, far, far, vmem, smem, vmem, vmem, vmem],
        out_specs=(far, far, far, far, vmem),
        scratch_shapes=[
            pltpu.VMEM((rows, kept, size, size), F32),
            pltpu.VMEM((rows, size, size), F32),
            pltpu.VMEM((rows, 2 * size, kept * size), BF16),
            pltpu.VMEM((rows, 2 * size, size), BF16),
            pltpu.VMEM((node_count, 4 * slots), BF16),
            pltpu.VMEM((2 * columns, node_count), BF16),
            pltpu.VMEM((rows, 2 * columns + 2 * agg, size), BF16),
            pltpu.VMEM((2 * agg, node_count), BF16),
            pltpu.VMEM((rows, size, 2 * size), BF16),
            held,
            held,
            held,
            held,
            held,
            held,
            pltpu.VMEM((rows, 5 * agg, size), F32),
            pltpu.VMEM((1, 4 * slots), F32),
            pltpu.VMEM((size, size), F32),
            pltpu.VMEM((5 * agg, n_coarse), F32),
            pltpu.VMEM((ITERS + 1, n_sub, agg, 2 * columns), F32),
            pltpu.VMEM((ITERS, 4, columns + agg, slots), F32),
            pltpu.VMEM((ITERS, 4, columns + agg, slots), F32),
            pltpu.SMEM((rows, kept), jnp.int32),
            dma((3,)),
            dma((rows,)),
            dma((4,)),
            dma((ITERS + 1,)),
            dma((ITERS + 1,)),
            dma((ITERS, 4)),
            dma((ITERS, 4)),
            dma((4,)),
            dma((4,)),
        ],
        compiler_params=pltpu.CompilerParams(
            collective_id=0, has_side_effects=True, vmem_limit_bytes=56 * 1024 * 1024
        ),
        cost_estimate=pl.CostEstimate(
            flops=4_000_000_000, bytes_accessed=12_000_000, transcendentals=0
        ),
    )(
        source_field,
        inject_amp.reshape(1, columns),
        inject_nodes,
        node_diag.reshape(1, node_count),
        blocks,
        pattern,
        local_inv,
        iface_nodes,
        iface_count,
        iface_wt,
        aggregate.reshape(1, node_count),
        coarse_inv,
    )
    step = step[:, :1]
    return x + step * u, r - step * w


def solution(mesh):
    in_specs = (
        P("groups", "sub"),
        P("groups"),
        P(None, "groups"),
        P("sub"),
        P("sub", None, None, None),
        P("sub", None),
        P("sub", None, None),
        P("sub", None, None),
        P("sub", None),
        P("sub", None, None),
        P("sub"),
        P("sub", None),
    )
    out_specs = (P("groups", "sub"), P("groups", "sub"))
    return jax.shard_map(shards, mesh=mesh, in_specs=in_specs, out_specs=out_specs, check_vma=False)
```

time: 61 us -> 50.3 us (0.82)
  Pallas kernels: 55 us -> 44.4 us
  local copies, waits for them, and re-layouts: 5.11 us -> 2.22 us
  other arithmetic: 0 us -> 2.69 us
    pallas_call x1, Pallas kernels: 55 us -> 44.4 us  [shards(): pl.pallas_call(kernel, out_shape=(field, field, field, field, jax.ShapeDt...]
    unnamed x3 -> x1, local copies, waits for them, and re-layouts: 5.11 us -> 1.36 us
    sub x0 -> x1, other arithmetic: none -> 2.69 us  [shards(): return (x + step * u, r - step * w)]
    slice x0 -> x1, local copies, waits for them, and re-layouts: none -> 0.86 us  [shards(): step = step[:, :1]]
where the time goes in v1:
time: 50.3 us; the launch traced here: 50 us
  Pallas kernels  44.4 us (88%)
  other arithmetic  2.69 us (5%)
  local copies, waits for them, and re-layouts  2.22 us (4%)
  between operations  0.64 us (1%)
    pallas_call x1, Pallas kernels, shards(): pl.pallas_call(kernel, out_shape=(field, field, field, field, jax.ShapeDt...  44.4 us
    sub x1, other arithmetic, shards(): return (x + step * u, r - step * w)  2.69 us
    unnamed x1, local copies, waits for them, and re-layouts  1.36 us

profile of v1, /device:TPU:0, one launch (start us, length us, event | category | flops | bytes accessed | tf_op | source)
XLA Modules:
  0.0 50.0 jit_solution(11796155334069145558)
XLA Ops:
  0.6 1.4 %copy.15.pattern_hbm = s32[16,7]{1,0:T(8,128)} copy(s32[16,7]{0,1:T(8,128)} %param.17) | data formatting | bytes 896 | tf_op args[5]
  2.0 44.4 %shard_map.131 = (f32[64,2048]{1,0:T(8,128)}, f32[64,2048]{1,0:T(8,128)}, f32[64,2048]{1,0:T(8,128)}, f32[64,2048]{1,0:T(8,128)}, f32[64,128]{1,0:T(8,128)}) custom-call(f32[64,2048]{1,0:T(8,128)} %source_hbm.1, f32[1,64]{1,0:T(1,128)} %bitcast.5, s32[2,64]{1,0:T(2,128)} %inject_ref.1, f32[1,2048]{1,0:T(1,128)} %bitcast.3, f32[16,7,128,128]{3,2,1,0:T(8,128)} %blocks_hbm.1, ...), custom_call_target="tpu_custom_call" | custom-call | flops 4000000000 | bytes 12000000 | tf_op jit(solution)/shard_map/pallas_call | solution.py:413
  46.4 0.9 %slice_reduce_fusion = f32[64]{0:T(128)S(1)} fusion(f32[64,128]{1,0:T(8,128)} %get-tuple-element.8), kind=kLoop, calls=%fused_computation.2 | loop fusion | bytes 512 | tf_op jit(solution)/shard_map/slice | solution.py:472
  47.3 2.7 %multiply_subtract_fusion = (f32[64,2048]{1,0:T(8,128)}, f32[64,2048]{1,0:T(8,128)}) fusion(f32[64,2048]{1,0:T(8,128)} %get-tuple-element.10, f32[64,2048]{1,0:T(8,128)} %get-tuple-element.11, f32[64]{0:T(128)S(1)} %slice_reduce_fusion, f32[64,2048]{1,0:T(8,128)} %get-tuple-element.7, f32[64,2048]{1,0:T(8,128)} %get-tuple-element.9), kind=kLoop, calls=%fused_computation | loop fusion | flops 524288 | bytes 3145984 | tf_op jit(solution)/shard_map/sub | solution.py:473

commit v2 on v1

--- a/solution.py
+++ b/solution.py
@@ -46,11 +46,8 @@
     weight_ref,
     aggregate_ref,
     coarse_ref,
-    x_hbm,
-    u_hbm,
-    r_hbm,
-    w_hbm,
-    step_ref,
+    x_now,
+    r_now,
     raw,
     raw_inv,
     mat,
@@ -61,9 +58,7 @@
     member,
     extra,
     local,
-    x_now,
     u_now,
-    r_now,
     w_now,
     y_now,
     ap,
@@ -76,7 +71,6 @@
     pattern_ref,
     load_sem,
     raw_sem,
-    out_sem,
     sum_send,
     sum_recv,
     face_send,
@@ -281,7 +275,7 @@
                 for k in range(kept):
                     mat[i, :, k * size : (k + 1) * size] = split(raw[i, k])
             picked = jnp.concatenate(
-                [split_l[pattern_ref[i, k], 0:depth, :] for k in range(kept)], axis=1
+                [split_l[pattern_ref[k, i], 0:depth, :] for k in range(kept)], axis=1
             )
             product = nt_dot(picked, mat[i])
             diag = diag_ref[:, at(i)]
@@ -365,14 +359,6 @@
 
     sums[ITERS, me] = jnp.concatenate([jnp.zeros((agg, columns), F32), dots_tile(dots)], axis=1)
     send_sums(ITERS)
-    leaving = [
-        pltpu.make_async_copy(held, out, out_sem.at[place])
-        for place, (held, out) in enumerate(
-            ((x_now, x_hbm), (u_now, u_hbm), (r_now, r_hbm), (w_now, w_hbm))
-        )
-    ]
-    for copy in leaving:
-        copy.start()
     for j in range(4):
         pl.when(there[j])(near_copy(j).wait_send)
         for stage in range(ITERS):
@@ -380,9 +366,14 @@
     for stage in range(ITERS + 1):
         all_sums(stage, sum_send).wait()
     all_sums(ITERS, sum_recv).wait()
-    step_ref[...] = step_of(ITERS)
-    for copy in leaving:
-        copy.wait()
+    step = step_of(ITERS)
+
+    def close(i, carry):
+        x_now[:, at(i)] = x_now[:, at(i)] + step * u_now[:, at(i)]
+        r_now[:, at(i)] = r_now[:, at(i)] - step * w_now[:, at(i)]
+        return carry
+
+    each(rows, close)
 
 
 def shards(
@@ -407,14 +398,13 @@
     vmem = pl.BlockSpec(memory_space=pltpu.VMEM)
     smem = pl.BlockSpec(memory_space=pltpu.SMEM)
     far = pl.BlockSpec(memory_space=pl.ANY)
-    field = jax.ShapeDtypeStruct((columns, node_count), F32)
     held = pltpu.VMEM((columns, node_count), F32)
     dma = pltpu.SemaphoreType.DMA
-    x, u, r, w, step = pl.pallas_call(
+    solution_out, residual_out = pl.pallas_call(
         kernel,
-        out_shape=(field, field, field, field, jax.ShapeDtypeStruct((columns, size), F32)),
+        out_shape=(held, held),
         in_specs=[far, vmem, vmem, vmem, far, far, far, vmem, smem, vmem, vmem, vmem],
-        out_specs=(far, far, far, far, vmem),
+        out_specs=(vmem, vmem),
         scratch_shapes=[
             pltpu.VMEM((rows, kept, size, size), F32),
             pltpu.VMEM((rows, size, size), F32),
@@ -429,8 +419,6 @@
             held,
             held,
             held,
-            held,
-            held,
             pltpu.VMEM((rows, 5 * agg, size), F32),
             pltpu.VMEM((1, 4 * slots), F32),
             pltpu.VMEM((size, size), F32),
@@ -438,10 +426,9 @@
             pltpu.VMEM((ITERS + 1, n_sub, agg, 2 * columns), F32),
             pltpu.VMEM((ITERS, 4, columns + agg, slots), F32),
             pltpu.VMEM((ITERS, 4, columns + agg, slots), F32),
-            pltpu.SMEM((rows, kept), jnp.int32),
+            pltpu.SMEM((kept, rows), jnp.int32),
             dma((3,)),
             dma((rows,)),
-            dma((4,)),
             dma((ITERS + 1,)),
             dma((ITERS + 1,)),
             dma((ITERS, 4)),
@@ -461,7 +448,7 @@
         inject_nodes,
         node_diag.reshape(1, node_count),
         blocks,
-        pattern,
+        pattern.T,
         local_inv,
         iface_nodes,
         iface_count,
@@ -469,8 +456,7 @@
         aggregate.reshape(1, node_count),
         coarse_inv,
     )
-    step = step[:, :1]
-    return x + step * u, r - step * w
+    return solution_out, residual_out
 
 
 def solution(mesh):

time: 50.3 us -> 46.3 us (0.920)
  other arithmetic: 2.69 us -> 0 us
  local copies, waits for them, and re-layouts: 2.22 us -> 1.59 us
    sub x1 -> x0, other arithmetic: 2.69 us -> none  [shards(): return (x + step * u, r - step * w)]
    slice x1 -> x0, local copies, waits for them, and re-layouts: 0.86 us -> none  [shards(): step = step[:, :1]]
    pallas_call x1, Pallas kernels: 44.4 us -> 43.9 us  [shards(): pl.pallas_call(kernel, out_shape=(held, held), in_specs=[far, vmem, vmem,...]
    unnamed x1 -> x2, local copies, waits for them, and re-layouts: 1.36 us -> 1.59 us
where the time goes in v2:
time: 46.3 us; the launch traced here: 46.1 us
  Pallas kernels  43.9 us (95%)
  local copies, waits for them, and re-layouts  1.59 us (3%)
  between operations  0.64 us (1%)
    pallas_call x1, Pallas kernels, shards(): pl.pallas_call(kernel, out_shape=(held, held), in_specs=[far, vmem, vmem,...  43.9 us
    unnamed x2, local copies, waits for them, and re-layouts  1.59 us

profile of v2, /device:TPU:0, one launch (start us, length us, event | category | flops | bytes accessed | tf_op | source)
XLA Modules:
  0.0 46.1 jit_solution(15552486900642897480)
XLA Ops:
  0.6 43.9 %shard_map.131 = (f32[64,2048]{1,0:T(8,128)S(1)}, f32[64,2048]{1,0:T(8,128)S(1)}) custom-call(f32[64,2048]{1,0:T(8,128)} %source_hbm.1, f32[1,64]{1,0:T(1,128)} %bitcast.7, s32[2,64]{1,0:T(2,128)} %inject_ref.1, f32[1,2048]{1,0:T(1,128)} %bitcast.4, f32[16,7,128,128]{3,2,1,0:T(8,128)} %blocks_hbm.1, s32[7,16]{1,0:T(8,128)} %bitcast.6, ...), custom_call_target="tpu_custom_call" | custom-call | flops 4000000000 | bytes 12000000 | tf_op jit(solution)/shard_map/pallas_call | solution.py:403
  44.5 0.8 %copy.16 = f32[64,2048]{1,0:T(8,128)} copy(f32[64,2048]{1,0:T(8,128)S(1)} %get-tuple-element.2) | data formatting | bytes 1048576
  45.3 0.8 %copy.17 = f32[64,2048]{1,0:T(8,128)} copy(f32[64,2048]{1,0:T(8,128)S(1)} %get-tuple-element.3) | data formatting | bytes 1048576

commit v3 on v2

--- a/solution.py
+++ b/solution.py
@@ -114,12 +114,12 @@
     source_copy = pltpu.make_async_copy(source_hbm, r_now, load_sem.at[0])
     inverse_copy = pltpu.make_async_copy(inverse_hbm, raw_inv, load_sem.at[1])
     pattern_copy = pltpu.make_async_copy(pattern_hbm, pattern_ref, load_sem.at[2])
+    others(greet)
     source_copy.start()
     inverse_copy.start()
     pattern_copy.start()
     for i in range(rows):
         block_copy(i).start()
-    others(greet)
 
     near_inv[0:agg, :] = coarse_ref[...]
 
@@ -232,7 +232,6 @@
 
     zero = jnp.zeros((columns, size), F32)
     dots = None
-    pl.semaphore_wait(barrier, n_sub - 1)
 
     for stage in range(ITERS):
         coarse = nt_dot(member[...], split_v[...])[:agg]
@@ -240,10 +239,9 @@
         sums[stage, me] = jnp.concatenate(
             [coarse[:, :columns] + coarse[:, columns:], beside], axis=1
         )
-        send_sums(stage)
-        if stage == 0:
-            for j in range(4):
-                pl.when(there[j])(near_copy(j).start)
+        if stage:
+            send_sums(stage)
+        else:
             inverse_copy.wait()
 
         def solve(i, carry):
@@ -255,6 +253,11 @@
             return carry
 
         each(rows, solve)
+        if stage == 0:
+            pl.semaphore_wait(barrier, n_sub - 1)
+            send_sums(stage)
+            for j in range(4):
+                pl.when(there[j])(near_copy(j).start)
 
         depth = double + 2 * agg if stage == 0 else double
         left = jnp.concatenate([split_l[i, 0:depth, :] for i in range(rows)], axis=1)

time: 46.3 us -> 46.7 us (level)
  no operation moved by 1% of the time
where the time goes in v3:
time: 46.7 us; the launch traced here: 46.5 us
  Pallas kernels  44.3 us (95%)
  local copies, waits for them, and re-layouts  1.59 us (3%)
  between operations  0.64 us (1%)
    pallas_call x1, Pallas kernels, shards(): pl.pallas_call(kernel, out_shape=(held, held), in_specs=[far, vmem, vmem,...  44.3 us
    unnamed x2, local copies, waits for them, and re-layouts  1.59 us

profile of v3, /device:TPU:0, one launch (start us, length us, event | category | flops | bytes accessed | tf_op | source)
XLA Modules:
  0.0 46.5 jit_solution(10192005883298039472)
XLA Ops:
  0.6 44.3 %shard_map.131 = (f32[64,2048]{1,0:T(8,128)S(1)}, f32[64,2048]{1,0:T(8,128)S(1)}) custom-call(f32[64,2048]{1,0:T(8,128)} %source_hbm.1, f32[1,64]{1,0:T(1,128)} %bitcast.7, s32[2,64]{1,0:T(2,128)} %inject_ref.1, f32[1,2048]{1,0:T(1,128)} %bitcast.4, f32[16,7,128,128]{3,2,1,0:T(8,128)} %blocks_hbm.1, s32[7,16]{1,0:T(8,128)} %bitcast.6, ...), custom_call_target="tpu_custom_call" | custom-call | flops 4000000000 | bytes 12000000 | tf_op jit(solution)/shard_map/pallas_call | solution.py:406
  45.0 0.8 %copy.16 = f32[64,2048]{1,0:T(8,128)} copy(f32[64,2048]{1,0:T(8,128)S(1)} %get-tuple-element.2) | data formatting | bytes 1048576
  45.8 0.8 %copy.17 = f32[64,2048]{1,0:T(8,128)} copy(f32[64,2048]{1,0:T(8,128)S(1)} %get-tuple-element.3) | data formatting | bytes 1048576
